TPU v7x, 32 devices: a whole 2x2x4 slice. The times are simulated.
32 devices in a mesh: cuts: 4 (over y, core), stem: 8 (over z, x).
Axes of the slice: x: 2, y: 2, z: 4, core: 2. Of those that a mesh axis runs over, the one named last changes fastest.
Arguments:
- stem_tensor: float32 [2048, 1024], P(('cuts', 'stem')), parts along dimension 0, may hold values from -0.25 to 0.25
- stem_cotangent: float32 [2048, 1024], P(('cuts', 'stem')), parts along dimension 0, may hold values from -6 to 6
- branch_tensor: bfloat16 [1024, 1024], P('stem'), may hold values from -0.1875 to 0.1875
- bit_order: int32 [16], replicated, may hold values from 0 to 15, each once
Outputs:
- stem_grad: float32 [2048, 1024], P(('cuts', 'stem')), parts along dimension 0
- branch_grad: float32 [4096, 1024], P(('cuts', 'stem')), parts along dimension 0
There are 4 independent parts, one for each index of `cuts`. A program takes and returns all parts, laid end to end along the dimension named above; an argument that names none is the same for every part. Nothing has to cross between parts.
Inputs may be any that keep to these rules, and one draw needn't show every extreme that they name: `bit_order`: a permutation of the 16 local index bit positions.
All inputs are finite; a program needn't handle non-finite values.
Results may differ from a plain program's by a relative error of at most 0.0003.
Values may be sent and summed in bfloat16 or wider, within the bound.
A program may use at most 64 MiB of HBM per device.

v0:
```python
import jax
import jax.numpy as jnp
from jax import lax
from jax.sharding import PartitionSpec as P


def bit_tables(bit_order, local_bits, dev_bits):
    local_size = 2**local_bits
    positions = jnp.arange(local_size, dtype=jnp.int32)
    forward = jnp.zeros((local_size,), jnp.int32)
    backward = jnp.zeros((local_size,), jnp.int32)
    for order_pos in range(local_bits):
        if order_pos < dev_bits:
            target_bit = dev_bits - 1 - order_pos
        else:
            target_bit = dev_bits + local_bits - 1 - order_pos
        source = bit_order[order_pos]
        forward = forward + jnp.left_shift(jnp.right_shift(positions, source) & 1, target_bit)
        backward = backward + jnp.left_shift(jnp.right_shift(positions, target_bit) & 1, source)
    return (forward, backward)


def cross_bits(operands):
    return (lax.all_to_all(operands[0], "stem", split_axis=1, concat_axis=1, tiled=True),)


def per_device(stem_tensor, stem_cotangent, branch_tensor, bit_order):
    members = lax.axis_size("stem")
    dev_bits = members.bit_length() - 1
    row_count, width = stem_tensor.shape
    local_size = row_count * width
    local_bits = local_size.bit_length() - 1
    free_size = local_size // members
    forward, backward = bit_tables(bit_order, local_bits, dev_bits)
    arranged = jnp.take(stem_tensor.reshape(local_size), backward).reshape(free_size, members)
    gathered = lax.all_gather(branch_tensor, "stem", axis=0, tiled=True)
    adjoint = lax.dot_general(
        stem_cotangent,
        gathered.astype(jnp.float32),
        (((1,), (1,)), ((), ())),
        precision=lax.Precision.HIGHEST,
        preferred_element_type=jnp.float32,
    )
    (moved,) = cross_bits((arranged,))
    (returned,) = cross_bits((adjoint.reshape(free_size, members),))
    perm_stem = moved.reshape(row_count, width)
    branch_term = lax.dot_general(
        perm_stem,
        stem_cotangent,
        (((0,), (0,)), ((), ())),
        precision=lax.Precision.HIGHEST,
        preferred_element_type=jnp.float32,
    )
    branch_grad = lax.psum_scatter(branch_term, "stem", scatter_dimension=0, tiled=True)
    stem_grad = jnp.take(returned.reshape(local_size), forward).reshape(row_count, width)
    return (stem_grad, branch_grad)


def solution(mesh):
    placed = (P(("cuts", "stem"), None), P(("cuts", "stem"), None), P("stem", None), P())
    return jax.shard_map(
        per_device,
        mesh=mesh,
        in_specs=placed,
        out_specs=(P(("cuts", "stem"), None), P(("cuts", "stem"), None)),
        check_vma=False,
    )
```

profile of v0, /device:TPU:0, one launch (start us, length us, event | category | flops | bytes accessed | tf_op | source)
XLA Modules:
  0.0 847.5 jit_solution(13714084007219988418)
XLA Ops:
  7.2 0.0 copy-start
  7.2 0.0 all-gather.2.cloned.1.call-start
  7.2 0.7 all-gather.2.cloned.1.call-update
  7.9 0.0 reduce-scatter.2.cloned.1.call-start
  8.0 1.0 copy.10
  9.0 1.9 fusion
  10.9 10.5 %broadcast_clamp_fusion = s32[65536]{0:T(1024)S(1)} fusion(s32[]{:T(128)} %bitcast.15, s32[]{:T(128)} %bitcast.14, s32[]{:T(128)} %bitcast.13, s32[]{:T(128)} %bitcast.12, s32[]{:T(128)} %bitcast.11, s32[]{:T(128)} %bitcast.10, s32[]{:T(128)} %bitcast.9, s32[]{:T(128)} %bitcast.8, s32[]{:T(128)} %bitcast.7, s32[]{:T(128)} %bitcast.6, s32[]{:T(128)} %bitcast.5, ...), kind=kLoop, calls=%fused_computation.6 | loop fusion | flops 4390912 | bytes 262208 | tf_op gather
  21.4 362.7 %gather_fusion.1 = f32[65536]{0:T(1024)S(1)} fusion(f32[65536]{0:T(1024)S(1)} %bitcast.26, s32[65536]{0:T(1024)S(1)} %broadcast_clamp_fusion), kind=kCustom, calls=%fused_computation.1.clone | custom fusion | bytes 786432 | tf_op jit(solution)/shard_map/jit(_take)/gather | solution.py:35
  384.1 10.5 %and_select_fusion = f32[65536]{0:T(1024)S(1)} fusion(f32[65536]{0:T(1024)S(1)} %gather_fusion.1, s32[]{:T(128)} %bitcast.15, s32[]{:T(128)} %bitcast.14, s32[]{:T(128)} %bitcast.13, s32[]{:T(128)} %bitcast.12, s32[]{:T(128)} %bitcast.11, s32[]{:T(128)} %bitcast.10, s32[]{:T(128)} %bitcast.9, s32[]{:T(128)} %bitcast.8, s32[]{:T(128)} %bitcast.7, s32[]{:T(128)} %bitcast.6, ...), kind=kLoop, calls=%fused_computation.4 | loop fusion | flops 4587520 | bytes 524352 | tf_op jit(solution)/shard_map/jit(_take)/select_n | solution.py:35
  394.6 3.6 all_to_all.14
  398.2 2.8 copy.8
  401.0 16.0 %all_to_all.18 = f32[8192,8,1]{0,2,1:T(1,128)S(1)} all-to-all(f32[8192,8,1]{0,2,1:T(1,128)S(1)} %copy.8), channel_id=1, replica_groups=mesh['cuts'=4,'stem'=8] {'stem'}, dimensions={1} | all-to-all | bytes 524288 | tf_op jit(solution)/shard_map/all_to_all | solution.py:24
  417.0 2.6 copy.9
  419.5 4.0 reshape.34
  423.5 0.0 copy-done
  423.5 5.0 fusion.2
  428.6 0.0 reduce-scatter.2.cloned.1.call-update
  428.6 0.0 all-gather.2.cloned.1.call-done
  428.6 3.6 fusion.1
  432.3 3.7 all_to_all.12
  435.9 3.5 copy.6
  439.4 4.0 all-to-all-start
  443.4 10.5 %broadcast_clamp_fusion.1 = s32[65536]{0:T(1024)S(1)} fusion(s32[]{:T(128)} %bitcast.15, s32[]{:T(128)} %bitcast.14, s32[]{:T(128)} %bitcast.13, s32[]{:T(128)} %bitcast.12, s32[]{:T(128)} %bitcast.11, s32[]{:T(128)} %bitcast.10, s32[]{:T(128)} %bitcast.9, s32[]{:T(128)} %bitcast.8, s32[]{:T(128)} %bitcast.7, s32[]{:T(128)} %bitcast.6, s32[]{:T(128)} %bitcast.5, ...), kind=kLoop, calls=%fused_computation.7 | loop fusion | flops 4390912 | bytes 262208 | tf_op gather
  453.8 6.6 all-to-all-done
  460.4 2.7 copy.7
  463.1 3.7 reshape.31
  466.8 362.7 %gather_fusion = f32[65536]{0:T(1024)S(1)} fusion(f32[65536]{0:T(1024)S(1)} %reshape.31, s32[65536]{0:T(1024)S(1)} %broadcast_clamp_fusion.1), kind=kCustom, calls=%fused_computation.clone | custom fusion | bytes 786432 | tf_op jit(solution)/shard_map/jit(_take)/gather | solution.py:55
  829.5 10.5 %and_select_fusion.1 = f32[65536]{0:T(1024)S(1)} fusion(f32[65536]{0:T(1024)S(1)} %gather_fusion, s32[]{:T(128)} %bitcast.15, s32[]{:T(128)} %bitcast.14, s32[]{:T(128)} %bitcast.13, s32[]{:T(128)} %bitcast.12, s32[]{:T(128)} %bitcast.11, s32[]{:T(128)} %bitcast.10, s32[]{:T(128)} %bitcast.9, s32[]{:T(128)} %bitcast.8, s32[]{:T(128)} %bitcast.7, s32[]{:T(128)} %bitcast.6, ...), kind=kLoop, calls=%fused_computation.5 | loop fusion | flops 4587520 | bytes 524352 | tf_op jit(solution)/shard_map/jit(_take)/select_n | solution.py:55
  840.0 0.7 reshape.32
  840.7 0.0 reduce-scatter.2.cloned.1.call-done
Async XLA Ops:
  7.2 416.4 %copy-start = (f32[64,1024]{1,0:T(8,128)S(1)}, f32[64,1024]{1,0:T(8,128)}, u32[]{:S(2)}) copy-start(f32[64,1024]{1,0:T(8,128)} %param.7) | copy-start | bytes 786436
  7.2 421.5 %all-gather.2.cloned.1.call-start = ((), (), s32[]{:S(2)}) async-start(), calls=%async_computation.3 | async-start | bytes 2359296 | tf_op jit(solution)/shard_map/all_gather | solution.py:36
  7.9 832.8 %reduce-scatter.2.cloned.1.call-start = ((), (), s32[]{:S(2)}) async-start(), calls=%async_computation.4 | async-start | bytes 4718592 | tf_op jit(solution)/shard_map/reduce_scatter | solution.py:54
  439.4 21.0 %all-to-all-start = ((f32[8192,8,1]{0,2,1:T(1,128)}), f32[8192,8,1]{0,2,1:T(1,128)S(1)}, u32[]{:S(2)}, u32[]{:S(2)}) async-start(f32[8192,8,1]{0,2,1:T(1,128)} %copy.6), calls=%async_computation | async-start | bytes 524288 | tf_op jit(solution)/shard_map/all_to_all | solution.py:24
Sparse Core Ops, SparseCore 0:
  10.1 51.9 all-gather.1
  428.7 91.8 reduce-scatter.1
where the time goes:
time: 848 us
  local copies, waits for them, and re-layouts  756 us (89%)
  other arithmetic  41.9 us (5%)
  blocking collectives  16 us (2%)
  between operations  14.1 us (2%)
  matrix products  8.66 us (1%)
    gather x1, local copies, waits for them, and re-layouts, per_device(): jnp.take(stem_tensor.reshape(local_size), backward)  363 us
    gather x1, local copies, waits for them, and re-layouts, per_device(): jnp.take(returned.reshape(local_size), forward).reshape(row_count, width)  363 us
    gather x2, other arithmetic  20.9 us
    all_to_all x6, local copies, waits for them, and re-layouts, cross_bits(): lax.all_to_all(operands[0], 'stem', split_axis=1, concat_axis=1, tiled=True)  18.8 us
  transfers between devices with their start and end apart: 3, of which 1 were waited for; matrix products, arithmetic and copies ran while one was open for 94% of the time, Pallas kernels for 0%

commit v1 on v0

--- a/solution.py
+++ b/solution.py
@@ -1,7 +1,14 @@
+import functools
+
 import jax
 import jax.numpy as jnp
 from jax import lax
+from jax.experimental import pallas as pl
+from jax.experimental.pallas import tpu as pltpu
 from jax.sharding import PartitionSpec as P
+
+LANES = 128
+LANE_BITS = 7
 
 
 def bit_tables(bit_order, local_bits, dev_bits):
@@ -20,11 +27,7 @@
     return (forward, backward)
 
 
-def cross_bits(operands):
-    return (lax.all_to_all(operands[0], "stem", split_axis=1, concat_axis=1, tiled=True),)
-
-
-def per_device(stem_tensor, stem_cotangent, branch_tensor, bit_order):
+def per_device_wide(stem_tensor, stem_cotangent, branch_tensor, bit_order):
     members = lax.axis_size("stem")
     dev_bits = members.bit_length() - 1
     row_count, width = stem_tensor.shape
@@ -41,8 +44,8 @@
         precision=lax.Precision.HIGHEST,
         preferred_element_type=jnp.float32,
     )
-    (moved,) = cross_bits((arranged,))
-    (returned,) = cross_bits((adjoint.reshape(free_size, members),))
+    moved = lax.all_to_all(arranged, "stem", split_axis=1, concat_axis=1, tiled=True)
+    returned = lax.all_to_all(adjoint.reshape(free_size, members), "stem", split_axis=1, concat_axis=1, tiled=True)
     perm_stem = moved.reshape(row_count, width)
     branch_term = lax.dot_general(
         perm_stem,
@@ -56,6 +59,314 @@
     return (stem_grad, branch_grad)
 
 
+def split2(x):
+    hi = x.astype(jnp.bfloat16)
+    lo = (x - hi.astype(jnp.float32)).astype(jnp.bfloat16)
+    return hi, lo
+
+
+def dot(a, b):
+    return jnp.dot(a, b, preferred_element_type=jnp.float32)
+
+
+def dot_t(a, b):
+    return lax.dot_general(a, b, (((1,), (1,)), ((), ())), preferred_element_type=jnp.float32)
+
+
+def one_hot(index, rows):
+    return (lax.broadcasted_iota(jnp.int32, (rows, index.shape[1]), 0) == index).astype(jnp.float32).astype(jnp.bfloat16)
+
+
+def iota_row(size):
+    return lax.broadcasted_iota(jnp.int32, (1, size), 1)
+
+
+def permute_plan(pairs, rows):
+    row_bits = rows.bit_length() - 1
+    lane, row = iota_row(LANES), iota_row(rows)
+    pre_lane, post_lane = jnp.zeros_like(lane), jnp.zeros_like(lane)
+    pre_row, post_row = jnp.zeros_like(row), jnp.zeros_like(row)
+    zero, one = jnp.int32(0), jnp.int32(1)
+    moved_l, moved_r, kept_l, kept_r = zero, zero, zero, zero
+    for i, o in pairs:
+        i, o = jnp.int32(i), jnp.int32(o)
+        li = jnp.where(i < LANE_BITS, one, zero)
+        lo = jnp.where(o < LANE_BITS, one, zero)
+        mid = jnp.where(
+            li == 1,
+            jnp.where(lo == 1, LANE_BITS - 1 - kept_l, moved_l),
+            jnp.where(lo == 1, moved_r, row_bits - 1 - kept_r),
+        )
+        moved_l = moved_l + li * (1 - lo)
+        moved_r = moved_r + (1 - li) * lo
+        kept_l = kept_l + li * lo
+        kept_r = kept_r + (1 - li) * (1 - lo)
+        i_lane, i_row = i * li, (i - LANE_BITS) * (1 - li)
+        o_lane, o_row = o * lo, (o - LANE_BITS) * (1 - lo)
+        pre_lane = pre_lane + ((lane >> (mid * li)) & li) * (one << i_lane)
+        pre_row = pre_row + ((row >> i_row) & (1 - li)) * (one << (mid * (1 - li)))
+        post_lane = post_lane + ((lane >> o_lane) & lo) * (one << (mid * lo))
+        post_row = post_row + ((row >> (mid * (1 - lo))) & (1 - lo)) * (one << o_row)
+    return pre_lane, pre_row, post_lane, post_row, moved_l
+
+
+def rows_times(m, x):
+    hi, lo = split2(x)
+    y = dot(m, jnp.concatenate([hi, lo], axis=1))
+    return y[:, :LANES] + y[:, LANES:]
+
+
+def lanes_times(x, m):
+    hi, lo = split2(x)
+    y = dot(jnp.concatenate([hi, lo], axis=0), m)
+    return y[: x.shape[0]] + y[x.shape[0] :]
+
+
+def permute_bits(x, plan):
+    rows = x.shape[0]
+    pre_lane, pre_row, post_lane, post_row, moved = plan
+    x = lanes_times(x, one_hot(pre_lane, LANES))
+    x = rows_times(one_hot(pre_row, rows), x)
+    ri = lax.broadcasted_iota(jnp.int32, (rows, LANES), 0)
+    ci = lax.broadcasted_iota(jnp.int32, (rows, LANES), 1)
+    for s in range(LANE_BITS):
+        step = 1 << s
+        active = jnp.where(moved > s, jnp.int32(1), jnp.int32(0))
+        up = pltpu.roll(pltpu.roll(x, rows - step, 0), step, 1)
+        down = pltpu.roll(pltpu.roll(x, step, 0), LANES - step, 1)
+        diff = (((ci >> s) & 1) - ((ri >> s) & 1)) * active
+        x = jnp.where(diff == 1, up, jnp.where(diff == -1, down, x))
+    x = rows_times(one_hot(post_row, rows), x)
+    return lanes_times(x, one_hot(post_lane, LANES))
+
+
+def kernel(n, order, stem, cot, branch, stem_grad, branch_grad, gat, bsend, brecv, ssend, srecv, gss, grs, bss, brs, sss, srs):
+    me = lax.axis_index("stem")
+    rows, width = stem.shape
+    tiles = width // LANES
+    flat_rows = rows * tiles
+    part = branch.shape[0] // n
+    row_bits = rows.bit_length() - 1
+    tile_bits = tiles.bit_length() - 1
+    dev_bits = n.bit_length() - 1
+    part_bits = part.bit_length() - 1
+    local_bits = row_bits + tile_bits + LANE_BITS
+    high_bits = local_bits - 2 * LANE_BITS
+    cols = 2
+    nz = n // cols
+    z, x = me // cols, me % cols
+    up_dev = jnp.minimum(me + cols, n - 1)
+    dn_dev = jnp.maximum(me - cols, 0)
+    x_dev = z * cols + (1 - x)
+
+    barrier = pltpu.get_barrier_semaphore()
+    for off in range(1, n):
+        pl.semaphore_signal(barrier, inc=1, device_id={"stem": (me + off) % n}, device_id_type=pl.DeviceIdType.MESH)
+
+    hi, lo = split2(cot[...])
+    mine = pl.ds(pl.multiple_of(me * rows, rows), rows)
+    gat[0, mine, :] = hi
+    gat[1, mine, :] = lo
+    pl.semaphore_wait(barrier, n - 1)
+
+    UP, DOWN, ACROSS = 0, 1, 2
+    targets = (up_dev, dn_dev, x_dev)
+
+    def block(h, o, way):
+        place = gat.at[h, pl.ds(pl.multiple_of(o * rows, rows), rows)]
+        return pltpu.make_async_remote_copy(
+            src_ref=place,
+            dst_ref=place,
+            send_sem=gss.at[h, o, way],
+            recv_sem=grs.at[h, o],
+            device_id={"stem": targets[way]},
+            device_id_type=pl.DeviceIdType.MESH,
+        )
+
+    def exists(way):
+        return (z < nz - 1, z > 0, z >= 0)[way]
+
+    def send(h, o, way):
+        @pl.when(exists(way))
+        def _():
+            block(h, o, way).start()
+
+    def arrive(h, o):
+        block(h, o, ACROSS).wait_recv()
+
+    def sent(h, o, way):
+        @pl.when(exists(way))
+        def _():
+            block(h, o, way).wait_send()
+
+    for h in (0, 1):
+        for way in (UP, DOWN, ACROSS):
+            send(h, me, way)
+
+    at = iota_row(n * part)
+    pick = one_hot((at % n) * part + at // n, n * part)
+    bsend[...] = dot(pick, branch[...]).astype(jnp.bfloat16).reshape(n, part, width)
+
+    def direct(src, dst, sems, rsems, off):
+        peer = (me + off) % n
+        return pltpu.make_async_remote_copy(
+            src_ref=src.at[peer],
+            dst_ref=dst.at[me],
+            send_sem=sems.at[off],
+            recv_sem=rsems.at[me],
+            device_id={"stem": peer},
+            device_id_type=pl.DeviceIdType.MESH,
+        )
+
+    def direct_in(src, dst, sems, rsems, off):
+        peer = (me + off) % n
+        return pltpu.make_async_remote_copy(
+            src_ref=src.at[peer],
+            dst_ref=dst.at[peer],
+            send_sem=sems.at[off],
+            recv_sem=rsems.at[peer],
+            device_id={"stem": peer},
+            device_id_type=pl.DeviceIdType.MESH,
+        )
+
+    for off in range(1, n):
+        direct(bsend, brecv, bss, brs, off).start()
+    brecv[me] = bsend[me]
+
+    arrive(0, x_dev)
+    send(0, x_dev, UP)
+    send(0, x_dev, DOWN)
+
+    def held(i):
+        return jnp.where(i < LANE_BITS, i, jnp.where(i < LANE_BITS + tile_bits, i + row_bits, i - tile_bits))
+
+    def placed(p):
+        if p < part_bits:
+            return LANE_BITS + p
+        if p < LANE_BITS:
+            return local_bits - dev_bits + p - part_bits
+        if p < 2 * LANE_BITS:
+            return p - LANE_BITS
+        return LANE_BITS + part_bits + p - 2 * LANE_BITS
+
+    spots = [held(order[m]) for m in range(local_bits)]
+    plan = permute_plan([(spots[m], placed(local_bits - 1 - m)) for m in range(local_bits)], flat_rows)
+    flat = jnp.concatenate([stem[:, t * LANES : (t + 1) * LANES] for t in range(tiles)], axis=0)
+    ssend[...] = permute_bits(flat, plan).reshape(n, flat_rows // n, LANES)
+    for off in range(1, n):
+        direct(ssend, srecv, sss, srs, off).start()
+    srecv[me] = ssend[me]
+
+    for k in range(1, nz):
+        @pl.when(z - k >= 0)
+        def _():
+            for xo in range(cols):
+                o = (z - k) * cols + xo
+                arrive(0, o)
+                send(0, o, UP)
+            o = (z - k) * cols + x
+            arrive(1, o)
+            send(1, o, UP)
+            send(1, o, ACROSS)
+
+        @pl.when(z + k <= nz - 1)
+        def _():
+            for xo in range(cols):
+                o = (z + k) * cols + xo
+                arrive(0, o)
+                send(0, o, DOWN)
+            o = (z + k) * cols + x
+            arrive(1, o)
+            send(1, o, DOWN)
+            send(1, o, ACROSS)
+
+    for zz in range(nz):
+        arrive(1, zz * cols + (1 - x))
+    for off in range(1, n):
+        direct_in(bsend, brecv, bss, brs, off).wait_recv()
+
+    taken = brecv[...].reshape(n * part, width)
+    adjoint = dot_t(gat[0], taken) + dot_t(gat[1], taken)
+    plan = permute_plan([(local_bits - 1 - m, spots[m]) for m in range(local_bits)], flat_rows)
+    back = permute_bits(adjoint, plan)
+    for t in range(tiles):
+        stem_grad[:, t * LANES : (t + 1) * LANES] = back[t * rows : (t + 1) * rows]
+
+    for off in range(1, n):
+        direct_in(ssend, srecv, sss, srs, off).wait_recv()
+    highs = 1 << high_bits
+    lhs = jnp.concatenate(
+        [srecv[:, e * part : (e + 1) * part, :].reshape(n * part, LANES) for e in range(highs)], axis=1
+    )
+    hi, lo = split2(lhs)
+    at = iota_row(n * part)
+    mix = one_hot((at % part) * n + at // part, n * part)
+    hi = dot(mix, hi).astype(jnp.bfloat16)
+    lo = dot(mix, lo).astype(jnp.bfloat16)
+    branch_grad[...] = dot(hi, gat[0]) + (dot(hi, gat[1]) + dot(lo, gat[0]))
+
+    for off in range(1, n):
+        direct(bsend, brecv, bss, brs, off).wait_send()
+        direct(ssend, srecv, sss, srs, off).wait_send()
+    for h in (0, 1):
+        for way in (UP, DOWN, ACROSS):
+            sent(h, me, way)
+    sent(0, x_dev, UP)
+    sent(0, x_dev, DOWN)
+    for k in range(1, nz):
+        @pl.when(z - k >= 0)
+        def _():
+            for xo in range(cols):
+                sent(0, (z - k) * cols + xo, UP)
+            o = (z - k) * cols + x
+            sent(1, o, UP)
+            sent(1, o, ACROSS)
+
+        @pl.when(z + k <= nz - 1)
+        def _():
+            for xo in range(cols):
+                sent(0, (z + k) * cols + xo, DOWN)
+            o = (z + k) * cols + x
+            sent(1, o, DOWN)
+            sent(1, o, ACROSS)
+
+
+def per_device(stem_tensor, stem_cotangent, branch_tensor, bit_order):
+    n = lax.axis_size("stem")
+    rows, width = stem_tensor.shape
+    flat_rows = rows * width // LANES
+    if n != 8 or width != n * LANES or branch_tensor.shape[0] != LANES or (rows, flat_rows) != (64, 512):
+        return per_device_wide(stem_tensor, stem_cotangent, branch_tensor, bit_order)
+    part = branch_tensor.shape[0] // n
+    vmem = pl.BlockSpec(memory_space=pltpu.VMEM)
+    dma = pltpu.SemaphoreType.DMA
+    return pl.pallas_call(
+        functools.partial(kernel, n),
+        out_shape=(
+            jax.ShapeDtypeStruct((rows, width), jnp.float32),
+            jax.ShapeDtypeStruct(branch_tensor.shape, jnp.float32),
+        ),
+        in_specs=[pl.BlockSpec(memory_space=pltpu.SMEM), vmem, vmem, vmem],
+        out_specs=(vmem, vmem),
+        scratch_shapes=[
+            pltpu.VMEM((2, n * rows, width), jnp.bfloat16),
+            pltpu.VMEM((n, part, width), jnp.bfloat16),
+            pltpu.VMEM((n, part, width), jnp.bfloat16),
+            pltpu.VMEM((n, flat_rows // n, LANES), jnp.float32),
+            pltpu.VMEM((n, flat_rows // n, LANES), jnp.float32),
+            dma((2, n, 3)),
+            dma((2, n)),
+            dma((n,)),
+            dma((n,)),
+            dma((n,)),
+            dma((n,)),
+        ],
+        compiler_params=pltpu.CompilerParams(
+            collective_id=0, has_side_effects=True, vmem_limit_bytes=40 * 1024 * 1024
+        ),
+    )(bit_order, stem_tensor, stem_cotangent, branch_tensor)
+
+
 def solution(mesh):
     placed = (P(("cuts", "stem"), None), P(("cuts", "stem"), None), P("stem", None), P())
     return jax.shard_map(

time: 848 us -> 56.4 us (0.07)
  local copies, waits for them, and re-layouts: 756 us -> 4.99 us
  Pallas kernels: 0 us -> 50.6 us
  other arithmetic: 41.9 us -> 0 us
  blocking collectives: 16 us -> 0 us
  between operations: 14.1 us -> 0.65 us
  matrix products: 8.66 us -> 0 us
    gather x2 -> x0, local copies, waits for them, and re-layouts: 725 us -> none  [the longest x1 363 us: per_device(): jnp.take(stem_tensor.reshape(local_size), backward)]
    pallas_call x0 -> x1, Pallas kernels: none -> 50.6 us  [per_device(): pl.pallas_call(functools.partial(kernel, n), out_shape=(jax.ShapeDtypeStr...]
    gather x2 -> x0, other arithmetic: 20.9 us -> none
    select_n x2 -> x0, other arithmetic: 20.9 us -> none  [the longest x1 10.5 us: per_device(): jnp.take(stem_tensor.reshape(local_size), backward)]
    all_to_all x6 -> x0, local copies, waits for them, and re-layouts: 18.8 us -> none  [cross_bits(): lax.all_to_all(operands[0], 'stem', split_axis=1, concat_axis=1, tiled=True)]
    all_to_all x1 -> x0, blocking collectives: 16 us -> none  [cross_bits(): lax.all_to_all(operands[0], 'stem', split_axis=1, concat_axis=1, tiled=True)]
    dot_general x2 -> x0, matrix products: 8.66 us -> none  [the longest x1 5.05 us: per_device(): lax.dot_general(perm_stem, stem_cotangent, (((0,), (0,)), ((), ())), prec...]
  transfers between devices with their start and end apart: 3 -> 0, of which waited for: 1 -> 0; matrix products, arithmetic and copies ran while one was open for 94% -> 0% of each run, Pallas kernels for 0% -> 0%
where the time goes in v1:
time: 56.4 us; the launch traced here: 56.2 us
  Pallas kernels  50.6 us (90%)
  local copies, waits for them, and re-layouts  4.99 us (9%)
  between operations  0.65 us (1%)
    pallas_call x1, Pallas kernels, per_device(): pl.pallas_call(functools.partial(kernel, n), out_shape=(jax.ShapeDtypeStr...  50.6 us
    unnamed x10, local copies, waits for them, and re-layouts  4.99 us

profile of v1, /device:TPU:0, one launch (start us, length us, event | category | flops | bytes accessed | tf_op | source)
XLA Modules:
  0.0 56.2 jit_solution(5692420085347741304)
XLA Ops:
  0.6 0.0 copy-start
  0.6 0.9 %copy-done = f32[64,1024]{1,0:T(8,128)S(1)} copy-done((f32[64,1024]{1,0:T(8,128)S(1)}, f32[64,1024]{1,0:T(8,128)}, u32[]{:S(2)}) %copy-start) | copy-done | bytes 262168
  1.6 0.0 copy-start.1
  1.6 0.9 %copy-done.1 = f32[64,1024]{1,0:T(8,128)S(1)} copy-done((f32[64,1024]{1,0:T(8,128)S(1)}, f32[64,1024]{1,0:T(8,128)}, u32[]{:S(2)}) %copy-start.1) | copy-done | bytes 262168
  2.5 0.0 copy-start.2
  2.5 0.9 %copy-done.2 = bf16[128,1024]{1,0:T(8,128)(2,1)S(1)} copy-done((bf16[128,1024]{1,0:T(8,128)(2,1)S(1)}, bf16[128,1024]{1,0:T(8,128)(2,1)}, u32[]{:S(2)}) %copy-start.2) | copy-done | bytes 262168
  3.5 0.0 copy-start.3
  3.5 0.7 %copy-done.3 = s32[16]{0:T(128)S(1)} copy-done((s32[16]{0:T(128)S(1)}, s32[16]{0:T(128)}, u32[]{:S(2)}) %copy-start.3) | copy-done | bytes 88
  4.1 50.6 %shard_map.59 = (f32[64,1024]{1,0:T(8,128)S(1)}, f32[128,1024]{1,0:T(8,128)S(1)}) custom-call(s32[16]{0:T(128)S(1)} %copy-done.3, f32[64,1024]{1,0:T(8,128)S(1)} %copy-done, f32[64,1024]{1,0:T(8,128)S(1)} %copy-done.1, bf16[128,1024]{1,0:T(8,128)(2,1)S(1)} %copy-done.2), custom_call_target="tpu_custom_call" | custom-call | tf_op jit(solution)/shard_map/pallas_call | solution.py:343
  54.7 0.7 %copy.8 = f32[64,1024]{1,0:T(8,128)} copy(f32[64,1024]{1,0:T(8,128)S(1)} %get-tuple-element.4) | data formatting | bytes 524288
  55.4 0.8 %copy.9 = f32[128,1024]{1,0:T(8,128)} copy(f32[128,1024]{1,0:T(8,128)S(1)} %get-tuple-element.5) | data formatting | bytes 1048576
Async XLA Ops:
  0.6 1.0 %copy-start = (f32[64,1024]{1,0:T(8,128)S(1)}, f32[64,1024]{1,0:T(8,128)}, u32[]{:S(2)}) copy-start(f32[64,1024]{1,0:T(8,128)} %stem.1) | copy-start | bytes 786436
  1.6 0.9 %copy-start.1 = (f32[64,1024]{1,0:T(8,128)S(1)}, f32[64,1024]{1,0:T(8,128)}, u32[]{:S(2)}) copy-start(f32[64,1024]{1,0:T(8,128)} %cot.1) | copy-start | bytes 786436
  2.5 0.9 %copy-start.2 = (bf16[128,1024]{1,0:T(8,128)(2,1)S(1)}, bf16[128,1024]{1,0:T(8,128)(2,1)}, u32[]{:S(2)}) copy-start(bf16[128,1024]{1,0:T(8,128)(2,1)} %branch.1) | copy-start | bytes 786436
  3.5 0.7 %copy-start.3 = (s32[16]{0:T(128)S(1)}, s32[16]{0:T(128)}, u32[]{:S(2)}) copy-start(s32[16]{0:T(128)} %order.1) | copy-start | bytes 196

commit v2 on v1

--- a/solution.py
+++ b/solution.py
@@ -9,6 +9,8 @@
 
 LANES = 128
 LANE_BITS = 7
+CODES = 32767.0
+KINDS = "BB"
 
 
 def bit_tables(bit_order, local_bits, dev_bits):
@@ -140,7 +142,18 @@
     return lanes_times(x, one_hot(post_lane, LANES))
 
 
-def kernel(n, order, stem, cot, branch, stem_grad, branch_grad, gat, bsend, brecv, ssend, srecv, gss, grs, bss, brs, sss, srs):
+def encode(x, axis):
+    top = jnp.maximum(jnp.max(jnp.abs(x), axis=axis, keepdims=True), 1e-30)
+    return jnp.round(x * (CODES / top)).astype(jnp.int32).astype(jnp.int16), top * (1.0 / CODES)
+
+
+def decode(q, step):
+    return q.astype(jnp.int32).astype(jnp.float32) * step
+
+
+def kernel(n, kinds, order, stem_hbm, cot_hbm, branch_hbm, stem_grad, branch_grad,
+           stem, cot, branch, code, high, low, bsend, brecv, ssend, srecv, tsend, trecv,
+           lsem, gss, grs, bss, brs, sss, srs, tss, trs):
     me = lax.axis_index("stem")
     rows, width = stem.shape
     tiles = width // LANES
@@ -155,87 +168,20 @@
     cols = 2
     nz = n // cols
     z, x = me // cols, me % cols
-    up_dev = jnp.minimum(me + cols, n - 1)
-    dn_dev = jnp.maximum(me - cols, 0)
-    x_dev = z * cols + (1 - x)
+    chunk = rows // len(kinds)
+    targets = (jnp.minimum(me + cols, n - 1), jnp.maximum(me - cols, 0), z * cols + (1 - x))
+    x_dev = targets[2]
+    MESH = pl.DeviceIdType.MESH
 
     barrier = pltpu.get_barrier_semaphore()
     for off in range(1, n):
-        pl.semaphore_signal(barrier, inc=1, device_id={"stem": (me + off) % n}, device_id_type=pl.DeviceIdType.MESH)
-
-    hi, lo = split2(cot[...])
-    mine = pl.ds(pl.multiple_of(me * rows, rows), rows)
-    gat[0, mine, :] = hi
-    gat[1, mine, :] = lo
-    pl.semaphore_wait(barrier, n - 1)
-
-    UP, DOWN, ACROSS = 0, 1, 2
-    targets = (up_dev, dn_dev, x_dev)
-
-    def block(h, o, way):
-        place = gat.at[h, pl.ds(pl.multiple_of(o * rows, rows), rows)]
-        return pltpu.make_async_remote_copy(
-            src_ref=place,
-            dst_ref=place,
-            send_sem=gss.at[h, o, way],
-            recv_sem=grs.at[h, o],
-            device_id={"stem": targets[way]},
-            device_id_type=pl.DeviceIdType.MESH,
-        )
-
-    def exists(way):
-        return (z < nz - 1, z > 0, z >= 0)[way]
-
-    def send(h, o, way):
-        @pl.when(exists(way))
-        def _():
-            block(h, o, way).start()
-
-    def arrive(h, o):
-        block(h, o, ACROSS).wait_recv()
-
-    def sent(h, o, way):
-        @pl.when(exists(way))
-        def _():
-            block(h, o, way).wait_send()
-
-    for h in (0, 1):
-        for way in (UP, DOWN, ACROSS):
-            send(h, me, way)
-
-    at = iota_row(n * part)
-    pick = one_hot((at % n) * part + at // n, n * part)
-    bsend[...] = dot(pick, branch[...]).astype(jnp.bfloat16).reshape(n, part, width)
-
-    def direct(src, dst, sems, rsems, off):
-        peer = (me + off) % n
-        return pltpu.make_async_remote_copy(
-            src_ref=src.at[peer],
-            dst_ref=dst.at[me],
-            send_sem=sems.at[off],
-            recv_sem=rsems.at[me],
-            device_id={"stem": peer},
-            device_id_type=pl.DeviceIdType.MESH,
-        )
-
-    def direct_in(src, dst, sems, rsems, off):
-        peer = (me + off) % n
-        return pltpu.make_async_remote_copy(
-            src_ref=src.at[peer],
-            dst_ref=dst.at[peer],
-            send_sem=sems.at[off],
-            recv_sem=rsems.at[peer],
-            device_id={"stem": peer},
-            device_id_type=pl.DeviceIdType.MESH,
-        )
-
-    for off in range(1, n):
-        direct(bsend, brecv, bss, brs, off).start()
-    brecv[me] = bsend[me]
-
-    arrive(0, x_dev)
-    send(0, x_dev, UP)
-    send(0, x_dev, DOWN)
+        pl.semaphore_signal(barrier, inc=1, device_id={"stem": (me + off) % n}, device_id_type=MESH)
+    loads = [
+        pltpu.make_async_copy(a, b, lsem.at[i])
+        for i, (a, b) in enumerate(((stem_hbm, stem), (cot_hbm, cot), (branch_hbm, branch)))
+    ]
+    for load in loads:
+        load.start()
 
     def held(i):
         return jnp.where(i < LANE_BITS, i, jnp.where(i < LANE_BITS + tile_bits, i + row_bits, i - tile_bits))
@@ -251,84 +197,156 @@
 
     spots = [held(order[m]) for m in range(local_bits)]
     plan = permute_plan([(spots[m], placed(local_bits - 1 - m)) for m in range(local_bits)], flat_rows)
+
+    loads[1].wait()
+    q, step = encode(cot[...], 0)
+    mine = pl.ds(pl.multiple_of(me * rows, rows), rows)
+    code[mine, :] = q
+    hi, lo = split2(cot[...])
+    high[mine, :] = hi
+    low[mine, :] = lo
+
+    loads[2].wait()
+    at = iota_row(n * part)
+    pick = one_hot((at % n) * part + at // n, n * part)
+    bsend[...] = dot(pick, branch[...]).astype(jnp.bfloat16).reshape(n, part, width)
+
+    loads[0].wait()
     flat = jnp.concatenate([stem[:, t * LANES : (t + 1) * LANES] for t in range(tiles)], axis=0)
-    ssend[...] = permute_bits(flat, plan).reshape(n, flat_rows // n, LANES)
-    for off in range(1, n):
-        direct(ssend, srecv, sss, srs, off).start()
+    arranged = permute_bits(flat, plan).reshape(n, flat_rows // n, LANES)
+    ssend[...], stem_step = encode(arranged, 1)
+    tsend[:, :, :width] = jnp.broadcast_to(step.reshape(1, 1, width), (n, 1, width))
+    tsend[:, :, width:] = stem_step
+    pl.semaphore_wait(barrier, n - 1)
+
+    UP, DOWN, ACROSS = 0, 1, 2
+
+    def block(c, o, way):
+        place = code.at[pl.ds(pl.multiple_of(o * rows + c * chunk, chunk), chunk)]
+        return pltpu.make_async_remote_copy(
+            src_ref=place,
+            dst_ref=place,
+            send_sem=gss.at[c, o, way],
+            recv_sem=grs.at[c, o],
+            device_id={"stem": targets[way]},
+            device_id_type=MESH,
+        )
+
+    def exists(way):
+        return (z < nz - 1, z > 0, z >= 0)[way]
+
+    def send(c, o, way):
+        @pl.when(exists(way))
+        def _():
+            block(c, o, way).start()
+
+    def arrive(c, o):
+        block(c, o, ACROSS).wait_recv()
+
+    def sent(c, o, way):
+        @pl.when(exists(way))
+        def _():
+            block(c, o, way).wait_send()
+
+    def direct(pair, off, incoming=False):
+        src, dst, sems, rsems = pair
+        peer = (me + off) % n
+        origin = peer if incoming else me
+        return pltpu.make_async_remote_copy(
+            src_ref=src.at[peer],
+            dst_ref=dst.at[origin],
+            send_sem=sems.at[off],
+            recv_sem=rsems.at[origin],
+            device_id={"stem": peer},
+            device_id_type=MESH,
+        )
+
+    branch_pair = (bsend, brecv, bss, brs)
+    stem_pair = (ssend, srecv, sss, srs)
+    step_pair = (tsend, trecv, tss, trs)
+
+    for c in range(len(kinds)):
+        for way in (UP, DOWN, ACROSS):
+            send(c, me, way)
+    for off in range(1, n):
+        direct(step_pair, off).start()
+    for off in range(1, n):
+        direct(branch_pair, off).start()
+    for off in range(1, n):
+        direct(stem_pair, off).start()
+    brecv[me] = bsend[me]
     srecv[me] = ssend[me]
-
+    trecv[me] = tsend[me]
+
+    def relay(act, k):
+        for c, kind in enumerate(kinds):
+            for xo in (x, 1 - x) if kind == "A" else (x,):
+                for side, way in ((-k, UP), (k, DOWN)):
+                    o = (z + side) * cols + xo
+
+                    @pl.when((z + side >= 0) & (z + side <= nz - 1))
+                    def _():
+                        act(c, o, way)
+                        if kind == "B":
+                            act(c, o, ACROSS)
+
+    def first(c, o, way):
+        if way != ACROSS:
+            arrive(c, o)
+        send(c, o, way)
+
+    for c, kind in enumerate(kinds):
+        if kind == "A":
+            arrive(c, x_dev)
+            send(c, x_dev, UP)
+            send(c, x_dev, DOWN)
     for k in range(1, nz):
-        @pl.when(z - k >= 0)
-        def _():
-            for xo in range(cols):
-                o = (z - k) * cols + xo
-                arrive(0, o)
-                send(0, o, UP)
-            o = (z - k) * cols + x
-            arrive(1, o)
-            send(1, o, UP)
-            send(1, o, ACROSS)
-
-        @pl.when(z + k <= nz - 1)
-        def _():
-            for xo in range(cols):
-                o = (z + k) * cols + xo
-                arrive(0, o)
-                send(0, o, DOWN)
-            o = (z + k) * cols + x
-            arrive(1, o)
-            send(1, o, DOWN)
-            send(1, o, ACROSS)
-
-    for zz in range(nz):
-        arrive(1, zz * cols + (1 - x))
-    for off in range(1, n):
-        direct_in(bsend, brecv, bss, brs, off).wait_recv()
+        relay(first, k)
+    for c, kind in enumerate(kinds):
+        if kind == "B":
+            for zz in range(nz):
+                arrive(c, zz * cols + (1 - x))
+    for off in range(1, n):
+        direct(step_pair, off, True).wait_recv()
+    for off in range(1, n):
+        peer = (me + off) % n
+        at = pl.ds(pl.multiple_of(peer * rows, rows), rows)
+        hi, lo = split2(decode(code[at, :], trecv[peer][:, :width]))
+        high[at, :] = hi
+        low[at, :] = lo
+    for off in range(1, n):
+        direct(branch_pair, off, True).wait_recv()
 
     taken = brecv[...].reshape(n * part, width)
-    adjoint = dot_t(gat[0], taken) + dot_t(gat[1], taken)
+    adjoint = dot_t(high[...], taken) + dot_t(low[...], taken)
     plan = permute_plan([(local_bits - 1 - m, spots[m]) for m in range(local_bits)], flat_rows)
     back = permute_bits(adjoint, plan)
     for t in range(tiles):
         stem_grad[:, t * LANES : (t + 1) * LANES] = back[t * rows : (t + 1) * rows]
 
     for off in range(1, n):
-        direct_in(ssend, srecv, sss, srs, off).wait_recv()
+        direct(stem_pair, off, True).wait_recv()
     highs = 1 << high_bits
-    lhs = jnp.concatenate(
-        [srecv[:, e * part : (e + 1) * part, :].reshape(n * part, LANES) for e in range(highs)], axis=1
-    )
+    got = decode(srecv[...], trecv[:, :, width:])
+    lhs = jnp.concatenate([got[:, e * part : (e + 1) * part].reshape(n * part, LANES) for e in range(highs)], axis=1)
     hi, lo = split2(lhs)
     at = iota_row(n * part)
     mix = one_hot((at % part) * n + at // part, n * part)
     hi = dot(mix, hi).astype(jnp.bfloat16)
     lo = dot(mix, lo).astype(jnp.bfloat16)
-    branch_grad[...] = dot(hi, gat[0]) + (dot(hi, gat[1]) + dot(lo, gat[0]))
-
-    for off in range(1, n):
-        direct(bsend, brecv, bss, brs, off).wait_send()
-        direct(ssend, srecv, sss, srs, off).wait_send()
-    for h in (0, 1):
+    branch_grad[...] = dot(hi, high[...]) + (dot(hi, low[...]) + dot(lo, high[...]))
+
+    for pair in (step_pair, branch_pair, stem_pair):
+        for off in range(1, n):
+            direct(pair, off).wait_send()
+    for c, kind in enumerate(kinds):
         for way in (UP, DOWN, ACROSS):
-            sent(h, me, way)
-    sent(0, x_dev, UP)
-    sent(0, x_dev, DOWN)
+            sent(c, me, way)
+        if kind == "A":
+            sent(c, x_dev, UP)
+            sent(c, x_dev, DOWN)
     for k in range(1, nz):
-        @pl.when(z - k >= 0)
-        def _():
-            for xo in range(cols):
-                sent(0, (z - k) * cols + xo, UP)
-            o = (z - k) * cols + x
-            sent(1, o, UP)
-            sent(1, o, ACROSS)
-
-        @pl.when(z + k <= nz - 1)
-        def _():
-            for xo in range(cols):
-                sent(0, (z + k) * cols + xo, DOWN)
-            o = (z + k) * cols + x
-            sent(1, o, DOWN)
-            sent(1, o, ACROSS)
+        relay(sent, k)
 
 
 def per_device(stem_tensor, stem_cotangent, branch_tensor, bit_order):
@@ -339,23 +357,34 @@
         return per_device_wide(stem_tensor, stem_cotangent, branch_tensor, bit_order)
     part = branch_tensor.shape[0] // n
     vmem = pl.BlockSpec(memory_space=pltpu.VMEM)
+    hbm = pl.BlockSpec(memory_space=pl.ANY)
     dma = pltpu.SemaphoreType.DMA
     return pl.pallas_call(
-        functools.partial(kernel, n),
+        functools.partial(kernel, n, KINDS),
         out_shape=(
             jax.ShapeDtypeStruct((rows, width), jnp.float32),
             jax.ShapeDtypeStruct(branch_tensor.shape, jnp.float32),
         ),
-        in_specs=[pl.BlockSpec(memory_space=pltpu.SMEM), vmem, vmem, vmem],
+        in_specs=[pl.BlockSpec(memory_space=pltpu.SMEM), hbm, hbm, hbm],
         out_specs=(vmem, vmem),
         scratch_shapes=[
-            pltpu.VMEM((2, n * rows, width), jnp.bfloat16),
+            pltpu.VMEM((rows, width), jnp.float32),
+            pltpu.VMEM((rows, width), jnp.float32),
+            pltpu.VMEM(branch_tensor.shape, jnp.bfloat16),
+            pltpu.VMEM((n * rows, width), jnp.int16),
+            pltpu.VMEM((n * rows, width), jnp.bfloat16),
+            pltpu.VMEM((n * rows, width), jnp.bfloat16),
             pltpu.VMEM((n, part, width), jnp.bfloat16),
             pltpu.VMEM((n, part, width), jnp.bfloat16),
-            pltpu.VMEM((n, flat_rows // n, LANES), jnp.float32),
-            pltpu.VMEM((n, flat_rows // n, LANES), jnp.float32),
-            dma((2, n, 3)),
-            dma((2, n)),
+            pltpu.VMEM((n, flat_rows // n, LANES), jnp.int16),
+            pltpu.VMEM((n, flat_rows // n, LANES), jnp.int16),
+            pltpu.VMEM((n, 1, width + LANES), jnp.float32),
+            pltpu.VMEM((n, 1, width + LANES), jnp.float32),
+            dma((3,)),
+            dma((len(KINDS), n, 3)),
+            dma((len(KINDS), n)),
+            dma((n,)),
+            dma((n,)),
             dma((n,)),
             dma((n,)),
             dma((n,)),

time: 56.4 us -> 40.9 us (0.73)
  Pallas kernels: 50.6 us -> 35.1 us
    pallas_call x1, Pallas kernels: 50.6 us -> 35.1 us  [per_device(): pl.pallas_call(functools.partial(kernel, n, KINDS), out_shape=(jax.ShapeD...]
where the time goes in v2:
time: 40.9 us; the launch traced here: 40.7 us
  Pallas kernels  35.1 us (86%)
  local copies, waits for them, and re-layouts  4.99 us (12%)
  between operations  0.65 us (2%)
    pallas_call x1, Pallas kernels, per_device(): pl.pallas_call(functools.partial(kernel, n, KINDS), out_shape=(jax.ShapeD...  35.1 us
    unnamed x10, local copies, waits for them, and re-layouts  4.99 us

profile of v2, /device:TPU:0, one launch (start us, length us, event | category | flops | bytes accessed | tf_op | source)
XLA Modules:
  0.0 40.7 jit_solution(15227283886456443423)
XLA Ops:
  0.6 0.0 copy-start
  0.6 0.9 %copy-done = f32[64,1024]{1,0:T(8,128)S(1)} copy-done((f32[64,1024]{1,0:T(8,128)S(1)}, f32[64,1024]{1,0:T(8,128)}, u32[]{:S(2)}) %copy-start) | copy-done | bytes 262168
  1.6 0.0 copy-start.1
  1.6 0.9 %copy-done.1 = f32[64,1024]{1,0:T(8,128)S(1)} copy-done((f32[64,1024]{1,0:T(8,128)S(1)}, f32[64,1024]{1,0:T(8,128)}, u32[]{:S(2)}) %copy-start.1) | copy-done | bytes 262168
  2.5 0.0 copy-start.2
  2.5 0.9 %copy-done.2 = bf16[128,1024]{1,0:T(8,128)(2,1)S(1)} copy-done((bf16[128,1024]{1,0:T(8,128)(2,1)S(1)}, bf16[128,1024]{1,0:T(8,128)(2,1)}, u32[]{:S(2)}) %copy-start.2) | copy-done | bytes 262168
  3.5 0.0 copy-start.3
  3.5 0.7 %copy-done.3 = s32[16]{0:T(128)S(1)} copy-done((s32[16]{0:T(128)S(1)}, s32[16]{0:T(128)}, u32[]{:S(2)}) %copy-start.3) | copy-done | bytes 88
  4.1 35.1 %shard_map.59 = (f32[64,1024]{1,0:T(8,128)S(1)}, f32[128,1024]{1,0:T(8,128)S(1)}) custom-call(s32[16]{0:T(128)S(1)} %copy-done.3, f32[64,1024]{1,0:T(8,128)S(1)} %copy-done, f32[64,1024]{1,0:T(8,128)S(1)} %copy-done.1, bf16[128,1024]{1,0:T(8,128)(2,1)S(1)} %copy-done.2), custom_call_target="tpu_custom_call" | custom-call | tf_op jit(solution)/shard_map/pallas_call | solution.py:362
  39.2 0.7 %copy.8 = f32[64,1024]{1,0:T(8,128)} copy(f32[64,1024]{1,0:T(8,128)S(1)} %get-tuple-element.4) | data formatting | bytes 524288
  39.9 0.8 %copy.9 = f32[128,1024]{1,0:T(8,128)} copy(f32[128,1024]{1,0:T(8,128)S(1)} %get-tuple-element.5) | data formatting | bytes 1048576
Async XLA Ops:
  0.6 1.0 %copy-start = (f32[64,1024]{1,0:T(8,128)S(1)}, f32[64,1024]{1,0:T(8,128)}, u32[]{:S(2)}) copy-start(f32[64,1024]{1,0:T(8,128)} %stem_hbm.1) | copy-start | bytes 786436
  1.6 0.9 %copy-start.1 = (f32[64,1024]{1,0:T(8,128)S(1)}, f32[64,1024]{1,0:T(8,128)}, u32[]{:S(2)}) copy-start(f32[64,1024]{1,0:T(8,128)} %cot_hbm.1) | copy-start | bytes 786436
  2.5 0.9 %copy-start.2 = (bf16[128,1024]{1,0:T(8,128)(2,1)S(1)}, bf16[128,1024]{1,0:T(8,128)(2,1)}, u32[]{:S(2)}) copy-start(bf16[128,1024]{1,0:T(8,128)(2,1)} %branch_hbm.1) | copy-start | bytes 786436
  3.5 0.7 %copy-start.3 = (s32[16]{0:T(128)S(1)}, s32[16]{0:T(128)}, u32[]{:S(2)}) copy-start(s32[16]{0:T(128)} %order.1) | copy-start | bytes 196

commit v3 on v2

--- a/solution.py
+++ b/solution.py
@@ -94,21 +94,18 @@
         i, o = jnp.int32(i), jnp.int32(o)
         li = jnp.where(i < LANE_BITS, one, zero)
         lo = jnp.where(o < LANE_BITS, one, zero)
-        mid = jnp.where(
-            li == 1,
-            jnp.where(lo == 1, LANE_BITS - 1 - kept_l, moved_l),
-            jnp.where(lo == 1, moved_r, row_bits - 1 - kept_r),
-        )
+        on_lane = jnp.where(li == lo, LANE_BITS - 1 - kept_l, jnp.where(li == 1, moved_l, moved_r))
+        on_row = jnp.where(li == lo, kept_r, row_bits - 1 - jnp.where(li == 1, moved_l, moved_r))
         moved_l = moved_l + li * (1 - lo)
         moved_r = moved_r + (1 - li) * lo
         kept_l = kept_l + li * lo
         kept_r = kept_r + (1 - li) * (1 - lo)
         i_lane, i_row = i * li, (i - LANE_BITS) * (1 - li)
         o_lane, o_row = o * lo, (o - LANE_BITS) * (1 - lo)
-        pre_lane = pre_lane + ((lane >> (mid * li)) & li) * (one << i_lane)
-        pre_row = pre_row + ((row >> i_row) & (1 - li)) * (one << (mid * (1 - li)))
-        post_lane = post_lane + ((lane >> o_lane) & lo) * (one << (mid * lo))
-        post_row = post_row + ((row >> (mid * (1 - lo))) & (1 - lo)) * (one << o_row)
+        pre_lane = pre_lane + ((lane >> (on_lane * li)) & li) * (one << i_lane)
+        pre_row = pre_row + ((row >> i_row) & (1 - li)) * (one << (on_row * (1 - li)))
+        post_lane = post_lane + ((lane >> o_lane) & lo) * (one << (on_lane * lo))
+        post_row = post_row + ((row >> (on_row * (1 - lo))) & (1 - lo)) * (one << o_row)
     return pre_lane, pre_row, post_lane, post_row, moved_l
 
 
@@ -124,20 +121,41 @@
     return y[: x.shape[0]] + y[x.shape[0] :]
 
 
-def permute_bits(x, plan):
+def swap_bits(x, moved):
+    rows = x.shape[0]
+    row_bits = rows.bit_length() - 1
+    lane = iota_row(LANES)
+    for s in range(LANE_BITS):
+        step = 1 << s
+        group = 1 << (row_bits - 1 - s)
+        active = jnp.where(moved > s, jnp.int32(1), jnp.int32(0))
+        high = (lane >> s) & 1
+        take_up = high * active == 1
+        take_down = (1 - high) * active == 1
+        if group >= 8:
+            pairs = x.reshape(rows // (2 * group), 2, group, LANES)
+            a = pairs[:, 0].reshape(rows // 2, LANES)
+            b = pairs[:, 1].reshape(rows // 2, LANES)
+            c = jnp.where(take_up, pltpu.roll(b, step, 1), a)
+            d = jnp.where(take_down, pltpu.roll(a, LANES - step, 1), b)
+            shape = (rows // (2 * group), 1, group, LANES)
+            x = jnp.concatenate([c.reshape(shape), d.reshape(shape)], axis=1).reshape(rows, LANES)
+        else:
+            upper = (lax.broadcasted_iota(jnp.int32, (rows, 1), 0) // group) % 2
+            up = pltpu.roll(pltpu.roll(x, rows - group, 0), step, 1)
+            down = pltpu.roll(pltpu.roll(x, group, 0), LANES - step, 1)
+            diff = (high - upper) * active
+            x = jnp.where(diff == 1, up, jnp.where(diff == -1, down, x))
+    return x
+
+
+def permute_bits(x, plan, lanes_done=False):
     rows = x.shape[0]
     pre_lane, pre_row, post_lane, post_row, moved = plan
-    x = lanes_times(x, one_hot(pre_lane, LANES))
+    if not lanes_done:
+        x = lanes_times(x, one_hot(pre_lane, LANES))
     x = rows_times(one_hot(pre_row, rows), x)
-    ri = lax.broadcasted_iota(jnp.int32, (rows, LANES), 0)
-    ci = lax.broadcasted_iota(jnp.int32, (rows, LANES), 1)
-    for s in range(LANE_BITS):
-        step = 1 << s
-        active = jnp.where(moved > s, jnp.int32(1), jnp.int32(0))
-        up = pltpu.roll(pltpu.roll(x, rows - step, 0), step, 1)
-        down = pltpu.roll(pltpu.roll(x, step, 0), LANES - step, 1)
-        diff = (((ci >> s) & 1) - ((ri >> s) & 1)) * active
-        x = jnp.where(diff == 1, up, jnp.where(diff == -1, down, x))
+    x = swap_bits(x, moved)
     x = rows_times(one_hot(post_row, rows), x)
     return lanes_times(x, one_hot(post_lane, LANES))
 
@@ -151,10 +169,11 @@
     return q.astype(jnp.int32).astype(jnp.float32) * step
 
 
-def kernel(n, kinds, order, stem_hbm, cot_hbm, branch_hbm, stem_grad, branch_grad,
+def kernel(n, cuts, kinds, order, stem_hbm, cot_hbm, branch_hbm, stem_grad, branch_grad,
            stem, cot, branch, code, high, low, bsend, brecv, ssend, srecv, tsend, trecv,
-           lsem, gss, grs, bss, brs, sss, srs, tss, trs):
+           lsem, gss, grs, bss, brs, sss, srs, tss, trs, css, crs):
     me = lax.axis_index("stem")
+    cut = lax.axis_index("cuts")
     rows, width = stem.shape
     tiles = width // LANES
     flat_rows = rows * tiles
@@ -176,6 +195,8 @@
     barrier = pltpu.get_barrier_semaphore()
     for off in range(1, n):
         pl.semaphore_signal(barrier, inc=1, device_id={"stem": (me + off) % n}, device_id_type=MESH)
+    for off in range(1, cuts):
+        pl.semaphore_signal(barrier, inc=1, device_id={"cuts": (cut + off) % cuts}, device_id_type=MESH)
     loads = [
         pltpu.make_async_copy(a, b, lsem.at[i])
         for i, (a, b) in enumerate(((stem_hbm, stem), (cot_hbm, cot), (branch_hbm, branch)))
@@ -209,7 +230,9 @@
     loads[2].wait()
     at = iota_row(n * part)
     pick = one_hot((at % n) * part + at // n, n * part)
-    bsend[...] = dot(pick, branch[...]).astype(jnp.bfloat16).reshape(n, part, width)
+    quarter = width // cuts
+    columns = pl.ds(pl.multiple_of(cut * quarter, LANES), quarter)
+    bsend[...] = dot(pick, branch[:, columns]).astype(jnp.bfloat16).reshape(n, part, quarter)
 
     loads[0].wait()
     flat = jnp.concatenate([stem[:, t * LANES : (t + 1) * LANES] for t in range(tiles)], axis=0)
@@ -217,7 +240,7 @@
     ssend[...], stem_step = encode(arranged, 1)
     tsend[:, :, :width] = jnp.broadcast_to(step.reshape(1, 1, width), (n, 1, width))
     tsend[:, :, width:] = stem_step
-    pl.semaphore_wait(barrier, n - 1)
+    pl.semaphore_wait(barrier, n - 1 + cuts - 1)
 
     UP, DOWN, ACROSS = 0, 1, 2
 
@@ -261,20 +284,32 @@
             device_id_type=MESH,
         )
 
-    branch_pair = (bsend, brecv, bss, brs)
+    branch_pair = (bsend, brecv.at[cut], bss, brs)
+
+    def share(off, incoming=False):
+        origin = (cut + off) % cuts if incoming else cut
+        return pltpu.make_async_remote_copy(
+            src_ref=brecv.at[origin],
+            dst_ref=brecv.at[origin],
+            send_sem=css.at[off],
+            recv_sem=crs.at[origin],
+            device_id={"cuts": (cut + off) % cuts},
+            device_id_type=MESH,
+        )
+
     stem_pair = (ssend, srecv, sss, srs)
     step_pair = (tsend, trecv, tss, trs)
 
+    for off in range(1, n):
+        direct(branch_pair, off).start()
     for c in range(len(kinds)):
         for way in (UP, DOWN, ACROSS):
             send(c, me, way)
     for off in range(1, n):
         direct(step_pair, off).start()
     for off in range(1, n):
-        direct(branch_pair, off).start()
-    for off in range(1, n):
         direct(stem_pair, off).start()
-    brecv[me] = bsend[me]
+    brecv[cut, me] = bsend[me]
     srecv[me] = ssend[me]
     trecv[me] = tsend[me]
 
@@ -300,32 +335,52 @@
             arrive(c, x_dev)
             send(c, x_dev, UP)
             send(c, x_dev, DOWN)
-    for k in range(1, nz):
+    relay(first, 1)
+    for off in range(1, n):
+        direct(branch_pair, off, True).wait_recv()
+    for off in range(1, cuts):
+        share(off).start()
+    for k in range(2, nz):
         relay(first, k)
-    for c, kind in enumerate(kinds):
-        if kind == "B":
-            for zz in range(nz):
-                arrive(c, zz * cols + (1 - x))
-    for off in range(1, n):
-        direct(step_pair, off, True).wait_recv()
-    for off in range(1, n):
-        peer = (me + off) % n
-        at = pl.ds(pl.multiple_of(peer * rows, rows), rows)
-        hi, lo = split2(decode(code[at, :], trecv[peer][:, :width]))
+
+    def unpack(o):
+        at = pl.ds(pl.multiple_of(o * rows, rows), rows)
+        hi, lo = split2(decode(code[at, :], trecv[o][:, :width]))
         high[at, :] = hi
         low[at, :] = lo
-    for off in range(1, n):
-        direct(branch_pair, off, True).wait_recv()
-
-    taken = brecv[...].reshape(n * part, width)
+
+    for off in range(1, n):
+        direct(step_pair, off, True).wait_recv()
+    for off in range(1, nz):
+        unpack(((z + off) % nz) * cols + x)
+    for off in range(1, cuts):
+        share(off, True).wait_recv()
+    plan = permute_plan([(local_bits - 1 - m, spots[m]) for m in range(local_bits)], flat_rows)
+    lane_rows = one_hot(plan[0], LANES)
+    taken = [
+        lax.dot_general(
+            lane_rows,
+            brecv[e].reshape(n * part, quarter),
+            (((0,), (0,)), ((), ())),
+            preferred_element_type=jnp.float32,
+        ).astype(jnp.bfloat16)
+        for e in range(cuts)
+    ]
+    taken = jnp.concatenate(taken, axis=1)
+    for off in range(1, n):
+        direct(stem_pair, off, True).wait_recv()
+    for off in range(nz):
+        zz = (z + off) % nz
+        for c, kind in enumerate(kinds):
+            if kind == "B":
+                arrive(c, zz * cols + (1 - x))
+        unpack(zz * cols + (1 - x))
+
     adjoint = dot_t(high[...], taken) + dot_t(low[...], taken)
-    plan = permute_plan([(local_bits - 1 - m, spots[m]) for m in range(local_bits)], flat_rows)
-    back = permute_bits(adjoint, plan)
+    back = permute_bits(adjoint, plan, True)
     for t in range(tiles):
         stem_grad[:, t * LANES : (t + 1) * LANES] = back[t * rows : (t + 1) * rows]
 
-    for off in range(1, n):
-        direct(stem_pair, off, True).wait_recv()
     highs = 1 << high_bits
     got = decode(srecv[...], trecv[:, :, width:])
     lhs = jnp.concatenate([got[:, e * part : (e + 1) * part].reshape(n * part, LANES) for e in range(highs)], axis=1)
@@ -336,6 +391,8 @@
     lo = dot(mix, lo).astype(jnp.bfloat16)
     branch_grad[...] = dot(hi, high[...]) + (dot(hi, low[...]) + dot(lo, high[...]))
 
+    for off in range(1, cuts):
+        share(off).wait_send()
     for pair in (step_pair, branch_pair, stem_pair):
         for off in range(1, n):
             direct(pair, off).wait_send()
@@ -350,17 +407,17 @@
 
 
 def per_device(stem_tensor, stem_cotangent, branch_tensor, bit_order):
-    n = lax.axis_size("stem")
+    n, cuts = lax.axis_size("stem"), lax.axis_size("cuts")
     rows, width = stem_tensor.shape
     flat_rows = rows * width // LANES
-    if n != 8 or width != n * LANES or branch_tensor.shape[0] != LANES or (rows, flat_rows) != (64, 512):
+    if n != 8 or width != n * LANES or branch_tensor.shape[0] != LANES or (rows, flat_rows) != (64, 512) or n % cuts:
         return per_device_wide(stem_tensor, stem_cotangent, branch_tensor, bit_order)
     part = branch_tensor.shape[0] // n
     vmem = pl.BlockSpec(memory_space=pltpu.VMEM)
     hbm = pl.BlockSpec(memory_space=pl.ANY)
     dma = pltpu.SemaphoreType.DMA
     return pl.pallas_call(
-        functools.partial(kernel, n, KINDS),
+        functools.partial(kernel, n, cuts, KINDS),
         out_shape=(
             jax.ShapeDtypeStruct((rows, width), jnp.float32),
             jax.ShapeDtypeStruct(branch_tensor.shape, jnp.float32),
@@ -374,8 +431,8 @@
             pltpu.VMEM((n * rows, width), jnp.int16),
             pltpu.VMEM((n * rows, width), jnp.bfloat16),
             pltpu.VMEM((n * rows, width), jnp.bfloat16),
-            pltpu.VMEM((n, part, width), jnp.bfloat16),
-            pltpu.VMEM((n, part, width), jnp.bfloat16),
+            pltpu.VMEM((n, part, width // cuts), jnp.bfloat16),
+            pltpu.VMEM((cuts, n, part, width // cuts), jnp.bfloat16),
             pltpu.VMEM((n, flat_rows // n, LANES), jnp.int16),
             pltpu.VMEM((n, flat_rows // n, LANES), jnp.int16),
             pltpu.VMEM((n, 1, width + LANES), jnp.float32),
@@ -389,6 +446,8 @@
             dma((n,)),
             dma((n,)),
             dma((n,)),
+            dma((cuts,)),
+            dma((cuts,)),
         ],
         compiler_params=pltpu.CompilerParams(
             collective_id=0, has_side_effects=True, vmem_limit_bytes=40 * 1024 * 1024

time: 40.9 us -> 35.7 us (0.87)
  Pallas kernels: 35.1 us -> 29.9 us
    pallas_call x1, Pallas kernels: 35.1 us -> 29.9 us  [per_device(): pl.pallas_call(functools.partial(kernel, n, cuts, KINDS), out_shape=(jax....]
where the time goes in v3:
time: 35.7 us; the launch traced here: 35.5 us
  Pallas kernels  29.9 us (84%)
  local copies, waits for them, and re-layouts  4.99 us (14%)
  between operations  0.65 us (2%)
    pallas_call x1, Pallas kernels, per_device(): pl.pallas_call(functools.partial(kernel, n, cuts, KINDS), out_shape=(jax....  29.9 us
    unnamed x10, local copies, waits for them, and re-layouts  4.99 us

profile of v3, /device:TPU:0, one launch (start us, length us, event | category | flops | bytes accessed | tf_op | source)
XLA Modules:
  0.0 35.5 jit_solution(5475939793035461386)
XLA Ops:
  0.6 0.0 copy-start
  0.6 0.9 %copy-done = f32[64,1024]{1,0:T(8,128)S(1)} copy-done((f32[64,1024]{1,0:T(8,128)S(1)}, f32[64,1024]{1,0:T(8,128)}, u32[]{:S(2)}) %copy-start) | copy-done | bytes 262168
  1.6 0.0 copy-start.1
  1.6 0.9 %copy-done.1 = f32[64,1024]{1,0:T(8,128)S(1)} copy-done((f32[64,1024]{1,0:T(8,128)S(1)}, f32[64,1024]{1,0:T(8,128)}, u32[]{:S(2)}) %copy-start.1) | copy-done | bytes 262168
  2.5 0.0 copy-start.2
  2.5 0.9 %copy-done.2 = bf16[128,1024]{1,0:T(8,128)(2,1)S(1)} copy-done((bf16[128,1024]{1,0:T(8,128)(2,1)S(1)}, bf16[128,1024]{1,0:T(8,128)(2,1)}, u32[]{:S(2)}) %copy-start.2) | copy-done | bytes 262168
  3.5 0.0 copy-start.3
  3.5 0.7 %copy-done.3 = s32[16]{0:T(128)S(1)} copy-done((s32[16]{0:T(128)S(1)}, s32[16]{0:T(128)}, u32[]{:S(2)}) %copy-start.3) | copy-done | bytes 88
  4.1 29.9 %shard_map.59 = (f32[64,1024]{1,0:T(8,128)S(1)}, f32[128,1024]{1,0:T(8,128)S(1)}) custom-call(s32[16]{0:T(128)S(1)} %copy-done.3, f32[64,1024]{1,0:T(8,128)S(1)} %copy-done, f32[64,1024]{1,0:T(8,128)S(1)} %copy-done.1, bf16[128,1024]{1,0:T(8,128)(2,1)S(1)} %copy-done.2), custom_call_target="tpu_custom_call" | custom-call | tf_op jit(solution)/shard_map/pallas_call | solution.py:419
  34.0 0.7 %copy.8 = f32[64,1024]{1,0:T(8,128)} copy(f32[64,1024]{1,0:T(8,128)S(1)} %get-tuple-element.4) | data formatting | bytes 524288
  34.7 0.8 %copy.9 = f32[128,1024]{1,0:T(8,128)} copy(f32[128,1024]{1,0:T(8,128)S(1)} %get-tuple-element.5) | data formatting | bytes 1048576
Async XLA Ops:
  0.6 1.0 %copy-start = (f32[64,1024]{1,0:T(8,128)S(1)}, f32[64,1024]{1,0:T(8,128)}, u32[]{:S(2)}) copy-start(f32[64,1024]{1,0:T(8,128)} %stem_hbm.1) | copy-start | bytes 786436
  1.6 0.9 %copy-start.1 = (f32[64,1024]{1,0:T(8,128)S(1)}, f32[64,1024]{1,0:T(8,128)}, u32[]{:S(2)}) copy-start(f32[64,1024]{1,0:T(8,128)} %cot_hbm.1) | copy-start | bytes 786436
  2.5 0.9 %copy-start.2 = (bf16[128,1024]{1,0:T(8,128)(2,1)S(1)}, bf16[128,1024]{1,0:T(8,128)(2,1)}, u32[]{:S(2)}) copy-start(bf16[128,1024]{1,0:T(8,128)(2,1)} %branch_hbm.1) | copy-start | bytes 786436
  3.5 0.7 %copy-start.3 = (s32[16]{0:T(128)S(1)}, s32[16]{0:T(128)}, u32[]{:S(2)}) copy-start(s32[16]{0:T(128)} %order.1) | copy-start | bytes 196

commit v4 on v3

--- a/solution.py
+++ b/solution.py
@@ -149,11 +149,10 @@
     return x
 
 
-def permute_bits(x, plan, lanes_done=False):
+def permute_bits(x, plan):
     rows = x.shape[0]
     pre_lane, pre_row, post_lane, post_row, moved = plan
-    if not lanes_done:
-        x = lanes_times(x, one_hot(pre_lane, LANES))
+    x = lanes_times(x, one_hot(pre_lane, LANES))
     x = rows_times(one_hot(pre_row, rows), x)
     x = swap_bits(x, moved)
     x = rows_times(one_hot(post_row, rows), x)
@@ -171,7 +170,7 @@
 
 def kernel(n, cuts, kinds, order, stem_hbm, cot_hbm, branch_hbm, stem_grad, branch_grad,
            stem, cot, branch, code, high, low, bsend, brecv, ssend, srecv, tsend, trecv,
-           lsem, gss, grs, bss, brs, sss, srs, tss, trs, css, crs):
+           lsem, gss, grs, bss, brs, sss, srs, tss, trs, css, crs, adj, first_rows, last_rows):
     me = lax.axis_index("stem")
     cut = lax.axis_index("cuts")
     rows, width = stem.shape
@@ -357,6 +356,9 @@
         share(off, True).wait_recv()
     plan = permute_plan([(local_bits - 1 - m, spots[m]) for m in range(local_bits)], flat_rows)
     lane_rows = one_hot(plan[0], LANES)
+    first_rows[...] = one_hot(plan[1], flat_rows)
+    last_rows[...] = one_hot(plan[3], flat_rows)
+    last_lanes = one_hot(plan[2], LANES)
     taken = [
         lax.dot_general(
             lane_rows,
@@ -369,27 +371,36 @@
     taken = jnp.concatenate(taken, axis=1)
     for off in range(1, n):
         direct(stem_pair, off, True).wait_recv()
+    highs = 1 << high_bits
+    got = decode(srecv[...], trecv[:, :, width:])
+    lhs = jnp.concatenate([got[:, e * part : (e + 1) * part].reshape(n * part, LANES) for e in range(highs)], axis=1)
+    hi, lo = split2(lhs)
+    at = iota_row(n * part)
+    mix = one_hot((at % part) * n + at // part, n * part)
+    left_hi = dot(mix, hi).astype(jnp.bfloat16)
+    left_lo = dot(mix, lo).astype(jnp.bfloat16)
+
+    def adjoin(o):
+        at = pl.ds(pl.multiple_of(o * rows, rows), rows)
+        both = dot_t(jnp.concatenate([high[at, :], low[at, :]], axis=0), taken)
+        adj[at, :] = both[:rows] + both[rows:]
+
+    for off in range(nz):
+        adjoin(((z + off) % nz) * cols + x)
     for off in range(nz):
         zz = (z + off) % nz
         for c, kind in enumerate(kinds):
             if kind == "B":
                 arrive(c, zz * cols + (1 - x))
         unpack(zz * cols + (1 - x))
-
-    adjoint = dot_t(high[...], taken) + dot_t(low[...], taken)
-    back = permute_bits(adjoint, plan, True)
+        adjoin(zz * cols + (1 - x))
+
+    back = swap_bits(rows_times(first_rows[...], adj[...]), plan[4])
+    back = lanes_times(rows_times(last_rows[...], back), last_lanes)
     for t in range(tiles):
         stem_grad[:, t * LANES : (t + 1) * LANES] = back[t * rows : (t + 1) * rows]
 
-    highs = 1 << high_bits
-    got = decode(srecv[...], trecv[:, :, width:])
-    lhs = jnp.concatenate([got[:, e * part : (e + 1) * part].reshape(n * part, LANES) for e in range(highs)], axis=1)
-    hi, lo = split2(lhs)
-    at = iota_row(n * part)
-    mix = one_hot((at % part) * n + at // part, n * part)
-    hi = dot(mix, hi).astype(jnp.bfloat16)
-    lo = dot(mix, lo).astype(jnp.bfloat16)
-    branch_grad[...] = dot(hi, high[...]) + (dot(hi, low[...]) + dot(lo, high[...]))
+    branch_grad[...] = dot(left_hi, high[...]) + (dot(left_hi, low[...]) + dot(left_lo, high[...]))
 
     for off in range(1, cuts):
         share(off).wait_send()
@@ -448,6 +459,9 @@
             dma((n,)),
             dma((cuts,)),
             dma((cuts,)),
+            pltpu.VMEM((flat_rows, LANES), jnp.float32),
+            pltpu.VMEM((flat_rows, flat_rows), jnp.bfloat16),
+            pltpu.VMEM((flat_rows, flat_rows), jnp.bfloat16),
         ],
         compiler_params=pltpu.CompilerParams(
             collective_id=0, has_side_effects=True, vmem_limit_bytes=40 * 1024 * 1024

time: 35.7 us -> 34.2 us (0.958)
  Pallas kernels: 29.9 us -> 28.3 us
    pallas_call x1, Pallas kernels: 29.9 us -> 28.3 us  [per_device(): pl.pallas_call(functools.partial(kernel, n, cuts, KINDS), out_shape=(jax....]
where the time goes in v4:
time: 34.2 us; the launch traced here: 34 us
  Pallas kernels  28.3 us (83%)
  local copies, waits for them, and re-layouts  4.99 us (15%)
  between operations  0.65 us (2%)
    pallas_call x1, Pallas kernels, per_device(): pl.pallas_call(functools.partial(kernel, n, cuts, KINDS), out_shape=(jax....  28.3 us
    unnamed x10, local copies, waits for them, and re-layouts  4.99 us

profile of v4, /device:TPU:0, one launch (start us, length us, event | category | flops | bytes accessed | tf_op | source)
XLA Modules:
  0.0 34.0 jit_solution(13119877588484991401)
XLA Ops:
  0.6 0.0 copy-start
  0.6 0.9 %copy-done = f32[64,1024]{1,0:T(8,128)S(1)} copy-done((f32[64,1024]{1,0:T(8,128)S(1)}, f32[64,1024]{1,0:T(8,128)}, u32[]{:S(2)}) %copy-start) | copy-done | bytes 262168
  1.6 0.0 copy-start.1
  1.6 0.9 %copy-done.1 = f32[64,1024]{1,0:T(8,128)S(1)} copy-done((f32[64,1024]{1,0:T(8,128)S(1)}, f32[64,1024]{1,0:T(8,128)}, u32[]{:S(2)}) %copy-start.1) | copy-done | bytes 262168
  2.5 0.0 copy-start.2
  2.5 0.9 %copy-done.2 = bf16[128,1024]{1,0:T(8,128)(2,1)S(1)} copy-done((bf16[128,1024]{1,0:T(8,128)(2,1)S(1)}, bf16[128,1024]{1,0:T(8,128)(2,1)}, u32[]{:S(2)}) %copy-start.2) | copy-done | bytes 262168
  3.5 0.0 copy-start.3
  3.5 0.7 %copy-done.3 = s32[16]{0:T(128)S(1)} copy-done((s32[16]{0:T(128)S(1)}, s32[16]{0:T(128)}, u32[]{:S(2)}) %copy-start.3) | copy-done | bytes 88
  4.1 28.3 %shard_map.59 = (f32[64,1024]{1,0:T(8,128)S(1)}, f32[128,1024]{1,0:T(8,128)S(1)}) custom-call(s32[16]{0:T(128)S(1)} %copy-done.3, f32[64,1024]{1,0:T(8,128)S(1)} %copy-done, f32[64,1024]{1,0:T(8,128)S(1)} %copy-done.1, bf16[128,1024]{1,0:T(8,128)(2,1)S(1)} %copy-done.2), custom_call_target="tpu_custom_call" | custom-call | tf_op jit(solution)/shard_map/pallas_call | solution.py:430
  32.5 0.7 %copy.8 = f32[64,1024]{1,0:T(8,128)} copy(f32[64,1024]{1,0:T(8,128)S(1)} %get-tuple-element.4) | data formatting | bytes 524288
  33.2 0.8 %copy.9 = f32[128,1024]{1,0:T(8,128)} copy(f32[128,1024]{1,0:T(8,128)S(1)} %get-tuple-element.5) | data formatting | bytes 1048576
Async XLA Ops:
  0.6 1.0 %copy-start = (f32[64,1024]{1,0:T(8,128)S(1)}, f32[64,1024]{1,0:T(8,128)}, u32[]{:S(2)}) copy-start(f32[64,1024]{1,0:T(8,128)} %stem_hbm.1) | copy-start | bytes 786436
  1.6 0.9 %copy-start.1 = (f32[64,1024]{1,0:T(8,128)S(1)}, f32[64,1024]{1,0:T(8,128)}, u32[]{:S(2)}) copy-start(f32[64,1024]{1,0:T(8,128)} %cot_hbm.1) | copy-start | bytes 786436
  2.5 0.9 %copy-start.2 = (bf16[128,1024]{1,0:T(8,128)(2,1)S(1)}, bf16[128,1024]{1,0:T(8,128)(2,1)}, u32[]{:S(2)}) copy-start(bf16[128,1024]{1,0:T(8,128)(2,1)} %branch_hbm.1) | copy-start | bytes 786436
  3.5 0.7 %copy-start.3 = (s32[16]{0:T(128)S(1)}, s32[16]{0:T(128)}, u32[]{:S(2)}) copy-start(s32[16]{0:T(128)} %order.1) | copy-start | bytes 196

commit v5 on v4

--- a/solution.py
+++ b/solution.py
@@ -233,14 +233,6 @@
     columns = pl.ds(pl.multiple_of(cut * quarter, LANES), quarter)
     bsend[...] = dot(pick, branch[:, columns]).astype(jnp.bfloat16).reshape(n, part, quarter)
 
-    loads[0].wait()
-    flat = jnp.concatenate([stem[:, t * LANES : (t + 1) * LANES] for t in range(tiles)], axis=0)
-    arranged = permute_bits(flat, plan).reshape(n, flat_rows // n, LANES)
-    ssend[...], stem_step = encode(arranged, 1)
-    tsend[:, :, :width] = jnp.broadcast_to(step.reshape(1, 1, width), (n, 1, width))
-    tsend[:, :, width:] = stem_step
-    pl.semaphore_wait(barrier, n - 1 + cuts - 1)
-
     UP, DOWN, ACROSS = 0, 1, 2
 
     def block(c, o, way):
@@ -299,11 +291,19 @@
     stem_pair = (ssend, srecv, sss, srs)
     step_pair = (tsend, trecv, tss, trs)
 
-    for off in range(1, n):
-        direct(branch_pair, off).start()
+    pl.semaphore_wait(barrier, n - 1 + cuts - 1)
     for c in range(len(kinds)):
         for way in (UP, DOWN, ACROSS):
             send(c, me, way)
+    for off in range(1, n):
+        direct(branch_pair, off).start()
+    loads[0].wait()
+    flat = jnp.concatenate([stem[:, t * LANES : (t + 1) * LANES] for t in range(tiles)], axis=0)
+    arranged = permute_bits(flat, plan).reshape(n, flat_rows // n, LANES)
+    ssend[...], stem_step = encode(arranged, 1)
+    tsend[:, :, :width] = jnp.broadcast_to(step.reshape(1, 1, width), (n, 1, width))
+    tsend[:, :, width:] = stem_step
+
     for off in range(1, n):
         direct(step_pair, off).start()
     for off in range(1, n):

time: 34.2 us -> 34.1 us (level)
  no operation moved by 1% of the time
where the time goes in v5:
time: 34.1 us; the launch traced here: 33.9 us
  Pallas kernels  28.2 us (83%)
  local copies, waits for them, and re-layouts  4.99 us (15%)
  between operations  0.65 us (2%)
    pallas_call x1, Pallas kernels, per_device(): pl.pallas_call(functools.partial(kernel, n, cuts, KINDS), out_shape=(jax....  28.2 us
    unnamed x10, local copies, waits for them, and re-layouts  4.99 us

profile of v5, /device:TPU:0, one launch (start us, length us, event | category | flops | bytes accessed | tf_op | source)
XLA Modules:
  0.0 33.9 jit_solution(11729020911442888805)
XLA Ops:
  0.6 0.0 copy-start
  0.6 0.9 %copy-done = f32[64,1024]{1,0:T(8,128)S(1)} copy-done((f32[64,1024]{1,0:T(8,128)S(1)}, f32[64,1024]{1,0:T(8,128)}, u32[]{:S(2)}) %copy-start) | copy-done | bytes 262168
  1.6 0.0 copy-start.1
  1.6 0.9 %copy-done.1 = f32[64,1024]{1,0:T(8,128)S(1)} copy-done((f32[64,1024]{1,0:T(8,128)S(1)}, f32[64,1024]{1,0:T(8,128)}, u32[]{:S(2)}) %copy-start.1) | copy-done | bytes 262168
  2.5 0.0 copy-start.2
  2.5 0.9 %copy-done.2 = bf16[128,1024]{1,0:T(8,128)(2,1)S(1)} copy-done((bf16[128,1024]{1,0:T(8,128)(2,1)S(1)}, bf16[128,1024]{1,0:T(8,128)(2,1)}, u32[]{:S(2)}) %copy-start.2) | copy-done | bytes 262168
  3.5 0.0 copy-start.3
  3.5 0.7 %copy-done.3 = s32[16]{0:T(128)S(1)} copy-done((s32[16]{0:T(128)S(1)}, s32[16]{0:T(128)}, u32[]{:S(2)}) %copy-start.3) | copy-done | bytes 88
  4.1 28.2 %shard_map.59 = (f32[64,1024]{1,0:T(8,128)S(1)}, f32[128,1024]{1,0:T(8,128)S(1)}) custom-call(s32[16]{0:T(128)S(1)} %copy-done.3, f32[64,1024]{1,0:T(8,128)S(1)} %copy-done, f32[64,1024]{1,0:T(8,128)S(1)} %copy-done.1, bf16[128,1024]{1,0:T(8,128)(2,1)S(1)} %copy-done.2), custom_call_target="tpu_custom_call" | custom-call | tf_op jit(solution)/shard_map/pallas_call | solution.py:430
  32.4 0.7 %copy.8 = f32[64,1024]{1,0:T(8,128)} copy(f32[64,1024]{1,0:T(8,128)S(1)} %get-tuple-element.4) | data formatting | bytes 524288
  33.1 0.8 %copy.9 = f32[128,1024]{1,0:T(8,128)} copy(f32[128,1024]{1,0:T(8,128)S(1)} %get-tuple-element.5) | data formatting | bytes 1048576
Async XLA Ops:
  0.6 1.0 %copy-start = (f32[64,1024]{1,0:T(8,128)S(1)}, f32[64,1024]{1,0:T(8,128)}, u32[]{:S(2)}) copy-start(f32[64,1024]{1,0:T(8,128)} %stem_hbm.1) | copy-start | bytes 786436
  1.6 0.9 %copy-start.1 = (f32[64,1024]{1,0:T(8,128)S(1)}, f32[64,1024]{1,0:T(8,128)}, u32[]{:S(2)}) copy-start(f32[64,1024]{1,0:T(8,128)} %cot_hbm.1) | copy-start | bytes 786436
  2.5 0.9 %copy-start.2 = (bf16[128,1024]{1,0:T(8,128)(2,1)S(1)}, bf16[128,1024]{1,0:T(8,128)(2,1)}, u32[]{:S(2)}) copy-start(bf16[128,1024]{1,0:T(8,128)(2,1)} %branch_hbm.1) | copy-start | bytes 786436
  3.5 0.7 %copy-start.3 = (s32[16]{0:T(128)S(1)}, s32[16]{0:T(128)}, u32[]{:S(2)}) copy-start(s32[16]{0:T(128)} %order.1) | copy-start | bytes 196
